TPU v7x, 256 devices: a whole 4x4x8 slice. The times are simulated.
256 devices in a mesh: dp: 16 (over y, x), dim: 16 (over z, core).
Axes of the slice: x: 4, y: 4, z: 8, core: 2. Of those that a mesh axis runs over, the one named last changes fastest.
Arguments:
- vectors: float32 [128, 65536], P('dim', 'dp'), may hold values from -192 to 192
- code_ids: int32 [8, 65536], P(None, 'dp'), may hold values from 0 to 255
- start_books: float32 [8, 128, 256], P(None, 'dim'), may hold values from -6 to 6
Outputs:
- codebooks: float32 [8, 128, 256], P(None, 'dim')
- residual: float32 [8, 128, 256], P(None, 'dim')
All inputs are finite; a program needn't handle non-finite values.
Results may differ from a plain program's by a relative error of at most 0.002.
Values sent between devices are 32-bit elements; how exact they have to be, the bound alone decides.
A program may use at most 64 MiB of HBM per device.

v0:
```python
import jax
import jax.numpy as jnp
from jax import lax
from jax.sharding import PartitionSpec as P

ITERS = 3


ridge = 0.5
highest = lax.Precision.HIGHEST


def project_rows(codebook, vectors, code_ids, subtract):
    sections = codebook.shape[0]
    width = codebook.shape[1]
    book_size = codebook.shape[2]
    row_count = code_ids.shape[1]
    block_len = 2048
    turn_count = row_count // block_len
    flat_book = jnp.transpose(codebook, (1, 0, 2)).reshape(width, sections * book_size)
    levels = lax.broadcasted_iota(jnp.int32, (1, book_size, 1), 1)

    def one_block(summed, position):
        start = position * block_len
        code_blk = lax.dynamic_slice_in_dim(code_ids, start, block_len, 1)
        onehot = (
            (code_blk[:, None, :] == levels)
            .astype(jnp.float32)
            .reshape(sections * book_size, block_len)
        )
        rebuilt = jnp.dot(flat_book, onehot, precision=highest, preferred_element_type=jnp.float32)
        if subtract:
            slab_part = lax.dynamic_slice_in_dim(vectors, start, block_len, 1)
            rebuilt = slab_part - rebuilt
        term = lax.dot_general(
            rebuilt,
            onehot,
            (((1,), (1,)), ((), ())),
            precision=highest,
            preferred_element_type=jnp.float32,
        )
        return (summed + term, None)

    summed, unused = lax.scan(
        one_block, jnp.zeros((width, sections * book_size), jnp.float32), jnp.arange(turn_count)
    )
    return jnp.transpose(summed.reshape(width, sections, book_size), (1, 0, 2))


def per_device(vectors, code_ids, start_books):
    row_count = code_ids.shape[1]
    scale = start_books.shape[2] / (row_count * lax.axis_size("dp"))

    def reduce_terms(terms):
        return scale * lax.psum(terms, "dp")

    def inner_one(left, right):
        return lax.psum(jnp.sum(left * right), "dim")

    solution = start_books
    residual = (
        reduce_terms(project_rows(start_books, vectors, code_ids, True)) - ridge * start_books
    )
    direction = residual
    norm_now = inner_one(residual, residual)
    for turn in range(ITERS):
        image = reduce_terms(project_rows(direction, vectors, code_ids, False)) + ridge * direction
        step_len = norm_now / inner_one(direction, image)
        solution = solution + step_len * direction
        residual = residual - step_len * image
        norm_next = inner_one(residual, residual)
        direction = residual + norm_next / norm_now * direction
        norm_now = norm_next
    return (solution, residual)


def solution(mesh):
    placed = (P("dim", "dp"), P(None, "dp"), P(None, "dim", None))
    return jax.shard_map(
        per_device,
        mesh=mesh,
        in_specs=placed,
        out_specs=(P(None, "dim", None), P(None, "dim", None)),
        check_vma=False,
    )
```

profile of v0, /device:TPU:1, one launch (start us, length us, event | category | flops | bytes accessed | tf_op | source)
XLA Modules:
  0.0 717.7 jit_solution(12498360289753820491)
XLA Ops:
  7.2 39.2 %while.44 = (s32[]{:T(128)}, f32[8,2048]{1,0:T(8,128)S(1)}, s32[2]{0:T(128)S(1)}, f32[8,4096]{1,0:T(8,128)}, s32[8,4096]{1,0:T(8,128)}, /*index=5*/f32[8,2048]{1...) while((s32[]{:T(128)}, f32[8,2048]{1,0:T(8,128)S(1)}, s32[2]{0:T(128)S(1)}, ...), condition=%wide.region_1.2_spmd.clone, body=%wide.region_0.1_spmd.clone.sunk | while | flops 809549824 | bytes 30769412 | solution.py:44
  9.4 3.0 bitcast_compare_fusion.8
  12.4 1.9 copy-done
  14.4 4.2 fusion.52
  18.5 8.3 %convolution_add_fusion.8 = f32[8,2048]{1,0:T(8,128)S(1)} fusion(f32[8,2048]{1,0:T(8,128)S(1)} %fusion.52, pred[2048,2048]{1,0:T(32,128)(4,1)} %copy-done, f32[8,2048]{1,0:T(8,128)S(1)} %get-tuple-element.413, pred[]{:T(512)S(6)} %compare.12), kind=kOutput, calls=%fused_computation.5.clone.1 | convolution fusion | flops 402685952 | bytes 4390913 | tf_op jit(solution)/shard_map/while/body/eval_jaxpr/dot_general | solution.py:35
  29.0 3.0 bitcast_compare_fusion.8
  32.0 1.9 copy-done
  33.9 4.2 fusion.52
  38.1 8.3 %convolution_add_fusion.8 = f32[8,2048]{1,0:T(8,128)S(1)} fusion(f32[8,2048]{1,0:T(8,128)S(1)} %fusion.52, pred[2048,2048]{1,0:T(32,128)(4,1)} %copy-done, f32[8,2048]{1,0:T(8,128)S(1)} %get-tuple-element.413, pred[]{:T(512)S(6)} %compare.12), kind=kOutput, calls=%fused_computation.5.clone.1 | convolution fusion | flops 402685952 | bytes 4390913 | tf_op jit(solution)/shard_map/while/body/eval_jaxpr/dot_general | solution.py:35
  47.3 93.2 %all-reduce.6.cloned.1.call-done = f32[8,8,256]{2,1,0:T(8,128)} async-done(((f32[8,8,256]{2,1,0:T(8,128)}), f32[8,8,256]{2,1,0:T(8,128)}) %all-reduce.6.cloned.1.call-update) | async-done | bytes 65552 | tf_op jit(solution)/shard_map/psum | solution.py:55
  141.4 52.1 %while.45 = (s32[]{:T(128)}, f32[8,2048]{1,0:T(8,128)S(1)}, s32[2]{0:T(128)S(1)}, s32[8,4096]{1,0:T(8,128)}, f32[8,2048]{1,0:T(8,128)S(1)}, /*index=5*/s32[]{:T(128)}, s32[1]{0:T(128)}, s32[]{:T(128)}, s32[]{:T(128)}) while((s32[]{:T(128)}, f32[8,2048]{1,0:T(8,128)S(1)}, s32[2]{0:T(128)S(1)}, s32[8,4096]{1,0:T(8,128)}, ...), condition=%wide.region_6.7_spmd.clone, body=%wide.region_5.6_spmd.clone.sunk | while | flops 813727744 | bytes 29917376 | solution.py:44
  143.5 3.0 bitcast_compare_fusion.9
  146.6 1.9 copy-done.1
  148.5 10.5 %fusion.57 = f32[2048,8]{1,0:T(8,128)S(1)} fusion(f32[8,2048]{1,0:T(8,128)S(1)} %get-tuple-element.454, pred[2048,2048]{1,0:T(32,128)(4,1)S(1)} %bitcast_compare_fusion.9), kind=kOutput, calls=%fused_computation.11.clone.1 | convolution fusion | flops 406847488 | bytes 4325376 | tf_op jit(solution)/shard_map/while/body/eval_jaxpr/dot_general | solution.py:31
  159.1 8.4 %convolution_add_fusion.9 = f32[8,2048]{1,0:T(8,128)S(1)} fusion(f32[2048,8]{1,0:T(8,128)S(1)} %fusion.57, pred[2048,2048]{1,0:T(32,128)(4,1)} %copy-done.1, f32[8,2048]{1,0:T(8,128)S(1)} %get-tuple-element.442, pred[]{:T(512)S(6)} %compare.13), kind=kOutput, calls=%fused_computation.13.clone.1 | convolution fusion | flops 402685952 | bytes 4390913 | tf_op jit(solution)/shard_map/while/body/eval_jaxpr/dot_general | solution.py:35
  169.6 3.0 bitcast_compare_fusion.9
  172.6 1.9 copy-done.1
  174.5 10.5 %fusion.57 = f32[2048,8]{1,0:T(8,128)S(1)} fusion(f32[8,2048]{1,0:T(8,128)S(1)} %get-tuple-element.454, pred[2048,2048]{1,0:T(32,128)(4,1)S(1)} %bitcast_compare_fusion.9), kind=kOutput, calls=%fused_computation.11.clone.1 | convolution fusion | flops 406847488 | bytes 4325376 | tf_op jit(solution)/shard_map/while/body/eval_jaxpr/dot_general | solution.py:31
  185.1 8.4 %convolution_add_fusion.9 = f32[8,2048]{1,0:T(8,128)S(1)} fusion(f32[2048,8]{1,0:T(8,128)S(1)} %fusion.57, pred[2048,2048]{1,0:T(32,128)(4,1)} %copy-done.1, f32[8,2048]{1,0:T(8,128)S(1)} %get-tuple-element.442, pred[]{:T(512)S(6)} %compare.13), kind=kOutput, calls=%fused_computation.13.clone.1 | convolution fusion | flops 402685952 | bytes 4390913 | tf_op jit(solution)/shard_map/while/body/eval_jaxpr/dot_general | solution.py:35
  194.2 90.6 %all-reduce.8.cloned.1.call-done = f32[8,8,256]{2,1,0:T(8,128)} async-done(((f32[8,8,256]{2,1,0:T(8,128)}), f32[8,8,256]{2,1,0:T(8,128)}) %all-reduce.8.cloned.1.call-update) | async-done | bytes 65552 | tf_op jit(solution)/shard_map/psum | solution.py:55
  284.8 1.5 multiply_reduce_fusion.4
  286.3 26.2 %all-reduce = (f32[]{:T(128)}, f32[]{:T(128)}) all-reduce(f32[]{:T(128)} %get-tuple-element.223, f32[]{:T(128)} %get-tuple-element.222), channel_id=1, replica_groups=mesh['dp'=16,'dim'=16] {'dim'}, use_global_device_ids=true, to_apply=%region_4.5 | all-reduce | flops 2 | bytes 16 | tf_op jit(solution)/shard_map/psum | solution.py:58
  315.3 25.1 %psum.74 = f32[]{:T(128)} all-reduce(f32[]{:T(128)} %multiply_reduce_fusion.3), channel_id=1, replica_groups=mesh['dp'=16,'dim'=16] {'dim'}, use_global_device_ids=true, to_apply=%region_11.12 | all-reduce | flops 1 | bytes 8 | tf_op jit(solution)/shard_map/psum | solution.py:58
  342.5 52.1 %while.46 = (s32[]{:T(128)}, f32[8,2048]{1,0:T(8,128)S(1)}, s32[2]{0:T(128)S(1)}, s32[8,4096]{1,0:T(8,128)}, f32[8,2048]{1,0:T(8,128)S(1)}, /*index=5*/s32[]{:T(128)}, s32[1]{0:T(128)}, s32[]{:T(128)}, s32[]{:T(128)}) while((s32[]{:T(128)}, f32[8,2048]{1,0:T(8,128)S(1)}, s32[2]{0:T(128)S(1)}, s32[8,4096]{1,0:T(8,128)}, ...), condition=%wide.region_13.14_spmd.clone, body=%wide.region_12.13_spmd.clone.sunk | while | flops 813727744 | bytes 29917376 | solution.py:44
  344.6 3.0 bitcast_compare_fusion.10
  347.7 1.9 copy-done.2
  349.6 10.5 %fusion.62 = f32[2048,8]{1,0:T(8,128)S(1)} fusion(f32[8,2048]{1,0:T(8,128)S(1)} %get-tuple-element.481, pred[2048,2048]{1,0:T(32,128)(4,1)S(1)} %bitcast_compare_fusion.10), kind=kOutput, calls=%fused_computation.17.clone.1 | convolution fusion | flops 406847488 | bytes 4325376 | tf_op jit(solution)/shard_map/while/body/eval_jaxpr/dot_general | solution.py:31
  360.2 8.4 %convolution_add_fusion.10 = f32[8,2048]{1,0:T(8,128)S(1)} fusion(f32[2048,8]{1,0:T(8,128)S(1)} %fusion.62, pred[2048,2048]{1,0:T(32,128)(4,1)} %copy-done.2, f32[8,2048]{1,0:T(8,128)S(1)} %get-tuple-element.469, pred[]{:T(512)S(6)} %compare.14), kind=kOutput, calls=%fused_computation.19.clone.1 | convolution fusion | flops 402685952 | bytes 4390913 | tf_op jit(solution)/shard_map/while/body/eval_jaxpr/dot_general | solution.py:35
  370.7 3.0 bitcast_compare_fusion.10
  373.7 1.9 copy-done.2
  375.6 10.5 %fusion.62 = f32[2048,8]{1,0:T(8,128)S(1)} fusion(f32[8,2048]{1,0:T(8,128)S(1)} %get-tuple-element.481, pred[2048,2048]{1,0:T(32,128)(4,1)S(1)} %bitcast_compare_fusion.10), kind=kOutput, calls=%fused_computation.17.clone.1 | convolution fusion | flops 406847488 | bytes 4325376 | tf_op jit(solution)/shard_map/while/body/eval_jaxpr/dot_general | solution.py:31
  386.2 8.4 %convolution_add_fusion.10 = f32[8,2048]{1,0:T(8,128)S(1)} fusion(f32[2048,8]{1,0:T(8,128)S(1)} %fusion.62, pred[2048,2048]{1,0:T(32,128)(4,1)} %copy-done.2, f32[8,2048]{1,0:T(8,128)S(1)} %get-tuple-element.469, pred[]{:T(512)S(6)} %compare.14), kind=kOutput, calls=%fused_computation.19.clone.1 | convolution fusion | flops 402685952 | bytes 4390913 | tf_op jit(solution)/shard_map/while/body/eval_jaxpr/dot_general | solution.py:35
  395.3 87.8 %all-reduce.10.cloned.1.call-done = f32[8,8,256]{2,1,0:T(8,128)} async-done(((f32[8,8,256]{2,1,0:T(8,128)}), f32[8,8,256]{2,1,0:T(8,128)}) %all-reduce.10.cloned.1.call-update) | async-done | bytes 65552 | tf_op jit(solution)/shard_map/psum | solution.py:55
  484.6 26.2 %psum.76 = f32[]{:T(128)} all-reduce(f32[]{:T(128)} %multiply_reduce_fusion.2), channel_id=1, replica_groups=mesh['dp'=16,'dim'=16] {'dim'}, use_global_device_ids=true, to_apply=%region_16.17 | all-reduce | flops 1 | bytes 8 | tf_op jit(solution)/shard_map/psum | solution.py:58
  512.1 1.5 multiply_reduce_fusion.1
  513.6 25.1 %psum.77 = f32[]{:T(128)} all-reduce(f32[]{:T(128)} %get-tuple-element.268), channel_id=1, replica_groups=mesh['dp'=16,'dim'=16] {'dim'}, use_global_device_ids=true, to_apply=%region_18.19 | all-reduce | flops 1 | bytes 8 | tf_op jit(solution)/shard_map/psum | solution.py:58
  540.0 52.1 %while.47 = (s32[]{:T(128)}, f32[8,2048]{1,0:T(8,128)S(1)}, s32[2]{0:T(128)S(1)}, s32[8,4096]{1,0:T(8,128)}, f32[8,2048]{1,0:T(8,128)S(1)}, /*index=5*/s32[]{:T(128)}, s32[1]{0:T(128)}, s32[]{:T(128)}, s32[]{:T(128)}) while((s32[]{:T(128)}, f32[8,2048]{1,0:T(8,128)S(1)}, s32[2]{0:T(128)S(1)}, s32[8,4096]{1,0:T(8,128)}, ...), condition=%wide.region_20.21_spmd.clone, body=%wide.region_19.20_spmd.clone.sunk | while | flops 813727744 | bytes 29917376 | solution.py:44
  542.1 3.0 bitcast_compare_fusion.11
  545.2 1.9 copy-done.3
  547.1 10.5 %fusion.67 = f32[2048,8]{1,0:T(8,128)S(1)} fusion(f32[8,2048]{1,0:T(8,128)S(1)} %get-tuple-element.508, pred[2048,2048]{1,0:T(32,128)(4,1)S(1)} %bitcast_compare_fusion.11), kind=kOutput, calls=%fused_computation.23.clone.1 | convolution fusion | flops 406847488 | bytes 4325376 | tf_op jit(solution)/shard_map/while/body/eval_jaxpr/dot_general | solution.py:31
  557.6 8.4 %convolution_add_fusion.11 = f32[8,2048]{1,0:T(8,128)S(1)} fusion(f32[2048,8]{1,0:T(8,128)S(1)} %fusion.67, pred[2048,2048]{1,0:T(32,128)(4,1)} %copy-done.3, f32[8,2048]{1,0:T(8,128)S(1)} %get-tuple-element.496, pred[]{:T(512)S(6)} %compare.15), kind=kOutput, calls=%fused_computation.25.clone.1 | convolution fusion | flops 402685952 | bytes 4390913 | tf_op jit(solution)/shard_map/while/body/eval_jaxpr/dot_general | solution.py:35
  568.1 3.0 bitcast_compare_fusion.11
  571.2 1.9 copy-done.3
  573.1 10.5 %fusion.67 = f32[2048,8]{1,0:T(8,128)S(1)} fusion(f32[8,2048]{1,0:T(8,128)S(1)} %get-tuple-element.508, pred[2048,2048]{1,0:T(32,128)(4,1)S(1)} %bitcast_compare_fusion.11), kind=kOutput, calls=%fused_computation.23.clone.1 | convolution fusion | flops 406847488 | bytes 4325376 | tf_op jit(solution)/shard_map/while/body/eval_jaxpr/dot_general | solution.py:31
  583.7 8.4 %convolution_add_fusion.11 = f32[8,2048]{1,0:T(8,128)S(1)} fusion(f32[2048,8]{1,0:T(8,128)S(1)} %fusion.67, pred[2048,2048]{1,0:T(32,128)(4,1)} %copy-done.3, f32[8,2048]{1,0:T(8,128)S(1)} %get-tuple-element.496, pred[]{:T(512)S(6)} %compare.15), kind=kOutput, calls=%fused_computation.25.clone.1 | convolution fusion | flops 402685952 | bytes 4390913 | tf_op jit(solution)/shard_map/while/body/eval_jaxpr/dot_general | solution.py:35
  592.7 87.9 %all-reduce.12.cloned.1.call-done = f32[8,8,256]{2,1,0:T(8,128)} async-done(((f32[8,8,256]{2,1,0:T(8,128)}), f32[8,8,256]{2,1,0:T(8,128)}) %all-reduce.12.cloned.1.call-update) | async-done | bytes 65552 | tf_op jit(solution)/shard_map/psum | solution.py:55
  682.1 26.2 %psum.79 = f32[]{:T(128)} all-reduce(f32[]{:T(128)} %multiply_reduce_fusion), channel_id=1, replica_groups=mesh['dp'=16,'dim'=16] {'dim'}, use_global_device_ids=true, to_apply=%region_23.24 | all-reduce | flops 1 | bytes 8 | tf_op jit(solution)/shard_map/psum | solution.py:58
  709.6 1.5 multiply_subtract_fusion
  (82 shorter events, 20.9 us)
Async XLA Ops:
  7.2 133.3 %all-reduce.6.cloned.1.call-start = ((), (), s32[]{:S(2)}) async-start(), calls=%async_computation | async-start | bytes 131072 | tf_op jit(solution)/shard_map/psum | solution.py:55
  7.2 7.1 copy-start.9
  7.3 7.1 copy-start.11
  12.4 1.9 copy-start
  26.8 7.1 copy-start.9
  26.8 7.1 copy-start.11
  32.0 1.9 copy-start
  46.4 0.6 copy-start.7
  47.1 237.7 %all-reduce.8.cloned.1.call-start = ((), (), s32[]{:S(2)}) async-start(), calls=%async_computation.1 | async-start | bytes 131072 | tf_op jit(solution)/shard_map/psum | solution.py:55
  146.6 1.9 copy-start.1
  172.6 1.9 copy-start.1
  193.5 0.7 copy-start.6
  194.2 289.0 %all-reduce.10.cloned.1.call-start = ((), (), s32[]{:S(2)}) async-start(), calls=%async_computation.2 | async-start | bytes 131072 | tf_op jit(solution)/shard_map/psum | solution.py:55
  342.5 169.6 %copy-start.8 = (f32[8,8,256]{2,1,0:T(8,128)S(1)}, f32[8,8,256]{2,1,0:T(8,128)}, u32[]{:S(2)}) copy-start(f32[8,8,256]{2,1,0:T(8,128)} %all-reduce.8.cloned.1.call-done) | copy-start | bytes 196612
  347.7 1.9 copy-start.2
  373.7 1.9 copy-start.2
  394.6 0.7 copy-start.4
  395.3 285.3 %all-reduce.12.cloned.1.call-start = ((), (), s32[]{:S(2)}) async-start(), calls=%async_computation.3 | async-start | bytes 131072 | tf_op jit(solution)/shard_map/psum | solution.py:55
  540.0 169.6 %copy-start.10 = (f32[8,2048]{1,0:T(8,128)S(1)}, f32[8,2048]{1,0:T(8,128)}, u32[]{:S(2)}) copy-start(f32[8,2048]{1,0:T(8,128)} %get-tuple-element.532) | copy-start | bytes 196612
  545.1 1.9 copy-start.3
  571.2 1.9 copy-start.3
  592.0 0.7 copy-start.5
Sparse Core Ops, SparseCore 0:
  47.2 93.2 all-reduce.5
  194.3 90.4 all-reduce.7
  395.4 87.7 all-reduce.9
  592.8 87.7 all-reduce.11
where the time goes:
time: 719 us; the launch traced here: 718 us
  waiting for transfers between devices  360 us (50%)
  matrix products  138 us (19%)
  blocking collectives  129 us (18%)
  other arithmetic  35 us (5%)
  local copies, waits for them, and re-layouts  29.7 us (4%)
  between operations  20.2 us (3%)
    psum x4, waiting for transfers between devices, reduce_terms(): return scale * lax.psum(terms, 'dp')  359 us
    psum x5, blocking collectives, inner_one(): return lax.psum(jnp.sum(left * right), 'dim')  129 us
    dot_general x8, matrix products, one_block(): jnp.dot(flat_book, onehot, precision=highest, preferred_element_type=jnp....  71.6 us
    dot_general x8, matrix products, one_block(): lax.dot_general(rebuilt, onehot, (((1,), (1,)), ((), ())), precision=high...  66.8 us
    eq x8, other arithmetic, one_block(): code_blk[:, None, :] == levels  24.4 us
    while x40, local copies, waits for them, and re-layouts  15.5 us
  transfers between devices with their start and end apart: 4, of which 4 were waited for; matrix products, arithmetic and copies ran while one was open for 0% of the time, Pallas kernels for 0%

commit v1 on v0

v1 whole, which is shorter than its diff:
```python
import functools

import jax
import jax.numpy as jnp
from jax import lax
from jax.experimental import pallas as pl
from jax.experimental.pallas import tpu as pltpu
from jax.sharding import PartitionSpec as P

f32 = jnp.float32
bf16 = jnp.bfloat16
MESH = pl.DeviceIdType.MESH
LANES = 128
SECTIONS = 8
CODES = 256
RIDGE = 0.5
SHIFT = 2.0


def two_sum(a, b):
    s = a + b
    t = s - a
    return s, (a - (s - t)) + (b - t)


def two_prod(a, b):
    p = a * b
    ca = a * 4097.0
    ah = ca - (ca - a)
    al = a - ah
    cb = b * 4097.0
    bh = cb - (cb - b)
    bl = b - bh
    return p, ((ah * bh - p) + ah * bl + al * bh) + al * bl


def tidy(h, r):
    s = h + r
    return s, r - (s - h)


def plus(a, b):
    s, e = two_sum(a[0], b[0])
    return tidy(s, e + (a[1] + b[1]))


def minus(a, b):
    return plus(a, (-b[0], -b[1]))


def times(a, b):
    p, e = two_prod(a[0], b[0])
    return tidy(p, e + (a[0] * b[1] + a[1] * b[0]))


def over(a, b):
    first = a[0] / b[0]
    rest = minus(a, times((first, jnp.zeros_like(first)), b))
    return tidy(first, rest[0] / b[0])


def scaled(a, power):
    return a[0] * power, a[1] * power


def pick(table, index):
    place = index & (LANES - 1)
    low = jnp.take_along_axis(table[0], place, axis=1)
    high = jnp.take_along_axis(table[1], place, axis=1)
    return jnp.where(index >= LANES, high, low)


def make_masks(ids_ref, low_ref, high_ref, chunk=1024):
    count = ids_ref.shape[1]
    row_low = lax.broadcasted_iota(jnp.int32, (64, chunk), 0) & 7
    row_high = lax.broadcasted_iota(jnp.int32, (CODES, chunk), 0) & 31

    def step(k, carry):
        span = pl.ds(pl.multiple_of(k * chunk, chunk), chunk)
        code = ids_ref[:, span]
        top = code >> 5
        wide = jnp.concatenate(
            [jnp.broadcast_to(top[m : m + 1], (8, chunk)) for m in range(SECTIONS)], axis=0
        )
        low_ref[:, span] = jnp.where(wide == row_low, 1.0, 0.0).astype(bf16)
        part = code & 31
        wide = jnp.concatenate(
            [jnp.broadcast_to(part[m : m + 1], (32, chunk)) for m in range(SECTIONS)], axis=0
        )
        high_ref[span, :] = jnp.where(wide == row_high, 1.0, 0.0).astype(bf16).T
        return carry

    lax.fori_loop(0, count // chunk, step, 0)


def forward_local(books_ref, vec_ref, ids_ref, e_ref):
    count = ids_ref.shape[1]

    def step(g, carry):
        span = pl.ds(pl.multiple_of(g * LANES, LANES), LANES)
        code = ids_ref[:, span]
        total = vec_ref[:, span]
        for m in range(SECTIONS):
            total = total - pick(
                (books_ref[0, 8 * m : 8 * m + 8, :], books_ref[1, 8 * m : 8 * m + 8, :]), jnp.broadcast_to(code[m : m + 1], (8, LANES))
            )
        e_ref[:, span] = total
        return carry

    lax.fori_loop(0, count // LANES, step, 0, unroll=4)


def forward(table, ids_ref, e_ref, packed=False):
    count = ids_ref.shape[1]
    row = lax.broadcasted_iota(jnp.int32, (8, LANES), 0)
    blocks = []
    table = (table[:, :LANES], table[:, LANES:])
    for g in range(count // LANES):
        span = slice(g * LANES, (g + 1) * LANES)
        e = jnp.sum(pick(table, ids_ref[:, span]), axis=0, keepdims=True)
        e_ref[:, span] = e
        if packed:
            wide = jnp.broadcast_to(e, (8, LANES))
            if g % 8 == 0:
                blocks.append(wide)
            else:
                blocks[-1] = jnp.where(row == g % 8, wide, blocks[-1])
    return blocks


def weighted(low, e_row):
    wide = jnp.broadcast_to(e_row, (16, e_row.shape[1]))
    first = wide.astype(bf16)
    second = (wide - first.astype(f32)).astype(bf16)
    return jnp.concatenate(
        [low * jnp.concatenate([first] * 4, axis=0), low * jnp.concatenate([second] * 4, axis=0)],
        axis=0,
    )


def backward(low_ref, high_ref, e_ref, size=2048):
    total = None
    for q in range(low_ref.shape[1] // size):
        span = slice(q * size, (q + 1) * size)
        rows = weighted(low_ref[:, span], e_ref[:, span])
        term = jnp.dot(rows, high_ref[span, :], preferred_element_type=f32)
        total = term if total is None else total + term
    return total


def extract(acc, fold_ref):
    both = acc[:64] + acc[64:]
    for m in range(SECTIONS):
        half = both[8 * m : 8 * m + 8, :LANES] if m < 4 else both[8 * m : 8 * m + 8, LANES:]
        fold_ref[8 * m : 8 * m + 8, :] = half if m % 4 == 0 else pltpu.roll(half, LANES - 32 * (m % 4), 1)
    block = lax.broadcasted_iota(jnp.int32, (8, LANES), 1) >> 5
    halves = []
    for h in range(2):
        out = None
        for q in range(4):
            piece = fold_ref[pl.ds(4 * h + q, 8, stride=8), :]
            out = piece if q == 0 else jnp.where(block == q, pltpu.roll(piece, 32 * q, 1), out)
        halves.append(out)
    return jnp.concatenate(halves, axis=1)


def dot_rows(pairs, extra):
    row = lax.broadcasted_iota(jnp.int32, (8, LANES), 0)
    found = []
    for a, b in pairs:
        left = two_prod(a[:, :LANES], b[:, :LANES])
        right = two_prod(a[:, LANES:], b[:, LANES:])
        found.append(scaled(plus(left, right), 0.5))
    found.append(extra)
    high = jnp.zeros((8, LANES), f32)
    rest = jnp.zeros((8, LANES), f32)
    for q, pair in enumerate(found):
        for distance in (4, 2, 1):
            pair = plus(pair, (pltpu.roll(pair[0], distance, 0), pltpu.roll(pair[1], distance, 0)))
        high = jnp.where(row == q, pair[0], high)
        rest = jnp.where(row == q, pair[1], rest)
    pair = (high, rest)
    for distance in (64, 32, 16, 8, 4, 2, 1):
        pair = plus(pair, (pltpu.roll(pair[0], distance, 1), pltpu.roll(pair[1], distance, 1)))
    return pair


def tree(terms):
    while len(terms) > 1:
        terms = [plus(terms[k], terms[k + 1]) for k in range(0, len(terms), 2)]
    return terms[0]


def solve(total, scale):
    d00, d01, d02, d11, d12, d22, norm = [(total[0][q : q + 1], total[1][q : q + 1]) for q in range(7)]
    w00 = plus(d01, scaled(d00, SHIFT))
    w01 = plus(d02, scaled(d01, SHIFT))
    w02 = plus(d12, scaled(d02, SHIFT))
    w11 = plus(d12, scaled(d11, SHIFT))
    w12 = plus(d22, scaled(d12, SHIFT))
    w22 = plus(scaled(norm, scale), scaled(d22, RIDGE))
    l1 = over(w01, w00)
    l2 = over(w02, w00)
    p1 = minus(w11, times(l1, w01))
    u12 = minus(w12, times(l2, w01))
    l3 = over(u12, p1)
    p2 = minus(minus(w22, times(l2, w02)), times(l3, u12))
    y1 = minus(d01, times(l1, d00))
    y2 = minus(minus(d02, times(l2, d00)), times(l3, y1))
    c2 = over(y2, p2)
    c1 = minus(over(y1, p1), times(l3, c2))
    c0 = minus(minus(over(d00, w00), times(l1, c1)), times(l2, c2))
    return c0, c1, c2


def kernel(
    planes, scale, vec_hbm, ids_hbm, books_hbm, x_ref, r_ref,
    vec, books, ids, low, high, e_local, e_rows, fold, acc,
    rs_out, rs_in, pair_out, pair_in, base, base_in, last_in,
    z_out, z_in, s_out, s_in,
    in_sem, ids_send, ids_recv, rs_send, rs_recv, pair_send, pair_recv,
    ag_send, ag_recv, z_send, z_recv, s_send, s_recv,
):
    dp = lax.axis_index("dp")
    dim = lax.axis_index("dim")
    core = dim % 2
    plane = dim // 2
    owner = dp // 8
    slot = dp % 8
    owned = core == owner
    half = ids.shape[2] // 2
    devices = 2 * planes

    def remote(src, dst, send_sem, recv_sem, target):
        return pltpu.make_async_remote_copy(
            src_ref=src, dst_ref=dst, send_sem=send_sem, recv_sem=recv_sem,
            device_id=target, device_id_type=MESH,
        )

    inputs = [
        pltpu.make_async_copy(ids_hbm, ids.at[8], in_sem.at[0]),
        pltpu.make_async_copy(books_hbm, books, in_sem.at[1]),
        pltpu.make_async_copy(vec_hbm, vec, in_sem.at[2]),
    ]
    for copy in inputs:
        copy.start()

    barrier = pltpu.get_barrier_semaphore()

    def greet_plane(k, carry):
        target = ((dp + k // 2) % 16, 2 * plane + (core + k) % 2)
        pl.semaphore_signal(barrier, inc=1, device_id=target, device_id_type=MESH)
        return carry

    def greet_line(k, carry):
        target = (dp, 2 * ((plane + k // 2) % planes) + k % 2)
        pl.semaphore_signal(barrier, inc=1, device_id=target, device_id_type=MESH)
        return carry

    lax.fori_loop(1, 32, greet_plane, 0)
    lax.fori_loop(2, devices, greet_line, 0)

    def ids_part(where, which):
        return ids.at[where, :, pl.ds(pl.multiple_of(which * half, half), half)]

    def ids_copy(k):
        return remote(
            ids_part(8, core), ids_part(slot, core), ids_send.at[k], ids_recv.at[slot, core],
            ((dp + k) % 16, 2 * plane + owner),
        )

    def ids_arrival(where, which):
        return remote(
            ids_part(8, which), ids_part(where, which), ids_send.at[0], ids_recv.at[where, which],
            (dp, 2 * plane + 1 - core),
        )

    def rs_copy(d, other):
        return remote(
            rs_out.at[d], rs_in.at[dp], rs_send.at[d, other], rs_recv.at[dp],
            (8 * core + d, 2 * plane + other),
        )

    def rs_away(d, other):
        return jnp.logical_or(8 * core + d != dp, other != core)

    def pair_copy(p):
        return remote(
            pair_out.at[p], pair_in.at[p], pair_send.at[p], pair_recv.at[p], (dp, 2 * plane + 1 - core)
        )

    def ag_copy(which, k):
        target = ((dp + k) % 16, dim)
        if which == 0:
            return remote(base.at[pl.ds(0, 3)], base_in.at[slot], ag_send.at[0, k], ag_recv.at[0, slot], target)
        return remote(base.at[3], last_in.at[slot], ag_send.at[1, k], ag_recv.at[1, slot], target)

    def ag_arrival(which, r):
        target = ((dp + 1) % 16, dim)
        if which == 0:
            return remote(base.at[pl.ds(0, 3)], base_in.at[r], ag_send.at[0, 0], ag_recv.at[0, r], target)
        return remote(base.at[3], last_in.at[r], ag_send.at[1, 0], ag_recv.at[1, r], target)

    def z_copy(k):
        return remote(z_out, z_in.at[dim], z_send.at[k], z_recv.at[dim], (dp, (dim + k) % devices))

    def z_arrival(k):
        return remote(z_out, z_in.at[k], z_send.at[0], z_recv.at[k], (dp, (dim + 1) % devices))

    def s_copy(k):
        return remote(s_out, s_in.at[dp], s_send.at[k], s_recv.at[dp], ((dp + k) % 16, dim))

    def s_arrival(k):
        return remote(s_out, s_in.at[k], s_send.at[0], s_recv.at[k], ((dp + 1) % 16, dim))

    def each(low_end, high_end, act):
        lax.fori_loop(low_end, high_end, lambda k, carry: (act(k), carry)[1], 0)

    def unless(skip, act):
        pl.when(jnp.logical_not(skip))(act)

    inputs[0].wait()
    make_masks(ids.at[8], low.at[8], high.at[8])
    inputs[1].wait()
    inputs[2].wait()
    forward_local(books, vec, ids.at[8], e_local)
    for d in range(8):
        e_rows[d] = e_local[d : d + 1, :]
        for h in range(2):
            rs_out[d, :, h * LANES : (h + 1) * LANES] = (RIDGE / 16) * books[h, pl.ds(d, 8, stride=8), :]

    pl.semaphore_wait(barrier, 31 + devices - 2)
    each(1, 16, lambda k: ids_copy(k).start())

    def local_pass(d, carry):
        found = extract(backward(low.at[8], high.at[8], e_rows.at[d]), fold)
        rs_out[d] = scale * found - rs_out[d]
        for other in range(2):
            pl.when(rs_away(d, other))(lambda: rs_copy(d, other).start())
        return carry

    lax.fori_loop(0, 8, local_pass, 0)

    @pl.when(owned)
    def _():
        rs_in[dp] = rs_out[slot]

    each(0, 16, lambda k: unless(jnp.logical_and(owned, k == dp), lambda: remote(
        rs_out.at[0], rs_in.at[k], rs_send.at[0, 0], rs_recv.at[k], (dp, 2 * plane + 1 - core)).wait_recv()))
    terms = [rs_in[k] for k in range(16)]
    while len(terms) > 1:
        terms = [terms[k] + terms[k + 1] for k in range(0, len(terms), 2)]
    base[0] = terms[0]

    def join(p, found):
        pair_out[p] = scale * found
        pair_copy(p).start()

    def joined(p):
        pair_copy(p).wait_recv()
        base[p + 1] = (pair_out[p] + pair_in[p]) + (RIDGE - SHIFT) * base[p]

    def place(q):
        return jnp.where(jnp.logical_and(owned, q == 0), 8, (slot + q) % 8)

    acc[...] = jnp.zeros_like(acc)

    def first_pass(q, carry):
        where = place(q)

        @pl.when(where < 8)
        def _():
            ids_arrival(where, 0).wait_recv()
            ids_arrival(where, 1).wait_recv()
            make_masks(ids.at[where], low.at[where], high.at[where])

        forward(base[0], ids.at[where], e_rows.at[q])
        acc[...] += backward(low.at[where], high.at[where], e_rows.at[q])
        return carry

    lax.fori_loop(0, 8, first_pass, 0)
    join(0, extract(acc[...], fold))
    joined(0)

    def sweep():
        def two(q, total):
            first, second = place(2 * q), place(2 * q + 1)
            one = backward(low.at[first], high.at[first], e_rows.at[2 * q])
            other = backward(low.at[second], high.at[second], e_rows.at[2 * q + 1])
            return total + (one + other)

        return lax.fori_loop(0, 4, two, jnp.zeros((128, CODES), f32))

    each(0, 8, lambda q: forward(base[1], ids.at[place(q)], e_rows.at[q]))
    join(1, extract(sweep(), fold))
    joined(1)

    @pl.when(owned)
    def _():
        each(1, 16, lambda k: ag_copy(0, k).start())
        base_in[slot] = base[0:3]

    def last_forward(q, carry):
        blocks = forward(base[2], ids.at[place(q)], e_rows.at[q], packed=True)
        for block in blocks:
            carry = plus(carry, two_prod(block, block))
        return carry

    zero = jnp.zeros((8, LANES), f32)
    norm = lax.fori_loop(0, 8, last_forward, (zero, zero))
    v0, v1, v2 = base[0], base[1], base[2]
    sums = dot_rows([(v0, v0), (v0, v1), (v0, v2), (v1, v1), (v1, v2), (v2, v2)], norm)
    z_out[0:8] = sums[0]
    z_out[8:16] = sums[1]
    each(1, devices, lambda k: z_copy(k).start())
    z_in[dim] = z_out[...]
    join(2, extract(sweep(), fold))
    each(0, devices, lambda k: unless(k == dim, lambda: z_arrival(k).wait_recv()))
    sums = tree([(z_in[k, 0:8], z_in[k, 8:16]) for k in range(devices)])
    s_out[0:8] = sums[0]
    s_out[8:16] = sums[1]
    each(1, 16, lambda k: s_copy(k).start())
    s_in[dp] = s_out[...]
    joined(2)

    @pl.when(owned)
    def _():
        each(1, 16, lambda k: ag_copy(1, k).start())
        last_in[slot] = base[3]

    each(0, 16, lambda k: unless(k == dp, lambda: s_arrival(k).wait_recv()))
    c0, c1, c2 = solve(tree([(s_in[k, 0:8], s_in[k, 8:16]) for k in range(16)]), scale)
    one = (jnp.ones_like(c0[0]), jnp.zeros_like(c0[0]))
    q0 = minus(one, scaled(c0, SHIFT))[0]
    q1 = -plus(c0, scaled(c1, SHIFT))[0]
    q2 = -plus(c1, scaled(c2, SHIFT))[0]
    q3 = -c2[0]
    c0, c1, c2 = c0[0], c1[0], c2[0]

    def arrived(which, r):
        unless(jnp.logical_and(owned, r == slot), lambda: ag_arrival(which, r).wait_recv())

    each(0, 8, lambda r: arrived(0, r))
    for d in range(8):
        for h in range(2):
            lanes = slice(h * LANES, (h + 1) * LANES)
            rows = pl.ds(d, 8, stride=8)
            v0, v1, v2 = [base_in[d, k, :, lanes] for k in range(3)]
            x_ref[h, rows, :] = books[h, rows, :] + (c0 * v0 + c1 * v1 + c2 * v2)
            base_in[d, 0, :, lanes] = q0 * v0 + q1 * v1 + q2 * v2
    each(0, 8, lambda r: arrived(1, r))
    for d in range(8):
        for h in range(2):
            lanes = slice(h * LANES, (h + 1) * LANES)
            r_ref[h, pl.ds(d, 8, stride=8), :] = base_in[d, 0, :, lanes] + q3 * last_in[d, :, lanes]

    each(1, 16, lambda k: ids_copy(k).wait_send())
    for other in range(2):
        each(0, 8, lambda d: pl.when(rs_away(d, other))(lambda: rs_copy(d, other).wait_send()))
    each(0, 3, lambda p: pair_copy(p).wait_send())
    each(1, devices, lambda k: z_copy(k).wait_send())
    each(1, 16, lambda k: s_copy(k).wait_send())

    @pl.when(owned)
    def _():
        each(1, 16, lambda k: ag_copy(0, k).wait_send())
        each(1, 16, lambda k: ag_copy(1, k).wait_send())


def per_device(planes, vectors, code_ids, start_books):
    sections, width, codes = start_books.shape
    count = code_ids.shape[1]
    scale = codes / (count * 16)
    devices = 2 * planes
    rows = sections * width
    books = jnp.transpose(start_books.reshape(rows, 2, LANES), (1, 0, 2))
    dma = pltpu.SemaphoreType.DMA
    halves = (2, rows, LANES)
    x, r = pl.pallas_call(
        functools.partial(kernel, planes, scale),
        out_shape=(jax.ShapeDtypeStruct(halves, f32),) * 2,
        in_specs=[pl.BlockSpec(memory_space=pl.ANY)] * 3,
        out_specs=(pl.BlockSpec(memory_space=pltpu.VMEM),) * 2,
        scratch_shapes=[
            pltpu.VMEM((width, count), f32),
            pltpu.VMEM(halves, f32),
            pltpu.VMEM((9, sections, count), jnp.int32),
            pltpu.VMEM((9, 64, count), bf16),
            pltpu.VMEM((9, count, CODES), bf16),
            pltpu.VMEM((width, count), f32),
            pltpu.VMEM((8, 1, count), f32),
            pltpu.VMEM((64, LANES), f32),
            pltpu.VMEM((128, CODES), f32),
            pltpu.VMEM((8, sections, CODES), f32),
            pltpu.VMEM((16, sections, CODES), f32),
            pltpu.VMEM((3, sections, CODES), f32),
            pltpu.VMEM((3, sections, CODES), f32),
            pltpu.VMEM((4, sections, CODES), f32),
            pltpu.VMEM((8, 3, sections, CODES), f32),
            pltpu.VMEM((8, sections, CODES), f32),
            pltpu.VMEM((16, LANES), f32),
            pltpu.VMEM((devices, 16, LANES), f32),
            pltpu.VMEM((16, LANES), f32),
            pltpu.VMEM((16, 16, LANES), f32),
            dma((3,)), dma((16,)), dma((8, 2)), dma((8, 2)), dma((16,)), dma((3,)), dma((3,)),
            dma((2, 16)), dma((2, 8)), dma((devices,)), dma((devices,)), dma((16,)), dma((16,)),
        ],
        compiler_params=pltpu.CompilerParams(
            collective_id=0, has_side_effects=True, vmem_limit_bytes=48 << 20
        ),
    )(vectors, code_ids, books)

    def back(array):
        return jnp.transpose(array, (1, 0, 2)).reshape(sections, width, codes)

    return back(x), back(r)


def solution(mesh):
    return jax.shard_map(
        functools.partial(per_device, mesh.shape["dim"] // 2),
        mesh=mesh,
        in_specs=(P("dim", "dp"), P(None, "dp"), P(None, "dim", None)),
        out_specs=(P(None, "dim", None), P(None, "dim", None)),
        check_vma=False,
    )
```

time: 719 us -> 65.9 us (0.09)
  waiting for transfers between devices: 360 us -> 0 us
  matrix products: 138 us -> 0 us
  blocking collectives: 129 us -> 0 us
  Pallas kernels: 0 us -> 62.7 us
  other arithmetic: 35 us -> 0 us
  local copies, waits for them, and re-layouts: 29.7 us -> 2.44 us
  between operations: 20.2 us -> 0.68 us
    psum x4 -> x0, waiting for transfers between devices: 359 us -> none  [reduce_terms(): return scale * lax.psum(terms, 'dp')]
    dot_general x16 -> x0, matrix products: 138 us -> none  [the longest x8 71.6 us: one_block(): jnp.dot(flat_book, onehot, precision=highest, preferred_element_type=jnp....]
    psum x5 -> x0, blocking collectives: 129 us -> none  [inner_one(): return lax.psum(jnp.sum(left * right), 'dim')]
    pallas_call x0 -> x1, Pallas kernels: none -> 62.7 us  [per_device(): pl.pallas_call(functools.partial(kernel, planes, scale), out_shape=(jax.S...]
    eq x8 -> x0, other arithmetic: 24.4 us -> none  [one_block(): code_blk[:, None, :] == levels]
    while x40 -> x0, local copies, waits for them, and re-layouts: 15.5 us -> none
    dynamic_slice x16 -> x0, local copies, waits for them, and re-layouts: 11.6 us -> none  [the longest x8 6.79 us: one_block(): code_blk = lax.dynamic_slice_in_dim(code_ids, start, block_len, 1)]
    reduce_sum x5 -> x0, other arithmetic: 7.33 us -> none  [inner_one(): return lax.psum(jnp.sum(left * right), 'dim')]
  transfers between devices with their start and end apart: 4 -> 0, of which waited for: 4 -> 0; matrix products, arithmetic and copies ran while one was open for 0% -> 0% of each run, Pallas kernels for 0% -> 0%
where the time goes in v1:
time: 65.9 us; the launch traced here: 65.8 us
  Pallas kernels  62.7 us (95%)
  local copies, waits for them, and re-layouts  2.44 us (4%)
  between operations  0.68 us (1%)
    pallas_call x1, Pallas kernels, per_device(): pl.pallas_call(functools.partial(kernel, planes, scale), out_shape=(jax.S...  62.7 us
    reshape x2, local copies, waits for them, and re-layouts, back(): return jnp.transpose(array, (1, 0, 2)).reshape(sections, width, codes)  1.37 us

profile of v1, /device:TPU:1, one launch (start us, length us, event | category | flops | bytes accessed | tf_op | source)
XLA Modules:
  0.0 65.8 jit_solution(2347092800115918034)
XLA Ops:
  0.6 0.0 copy-start.1
  0.6 0.0 copy-start
  0.6 0.9 %reshape.13 = f32[64,2,128]{2,1,0:T(2,128)S(1)} reshape(f32[8,8,256]{2,1,0:T(8,128)} %param.5) | data formatting | bytes 131072 | tf_op jit(solution)/shard_map/reshape | solution.py:476
  1.6 0.0 copy-done.1
  1.6 0.0 copy-done
  1.6 62.7 %shard_map.50 = (f32[2,64,128]{2,1,0:T(8,128)S(1)}, f32[2,64,128]{2,1,0:T(8,128)S(1)}) custom-call(f32[8,4096]{1,0:T(8,128)S(1)} %copy-done, s32[8,4096]{1,0:T(8,128)S(1)} %copy-done.1, f32[2,64,128]{2,1,0:T(8,128)S(1)} %bitcast.5), custom_call_target="tpu_custom_call" | custom-call | tf_op jit(solution)/shard_map/pallas_call | solution.py:479
  64.3 0.1 copy.6
  64.4 0.7 %reshape.14 = f32[8,8,256]{2,1,0:T(8,128)} reshape(f32[64,2,128]{2,1,0:T(2,128)S(1)} %copy.6) | data formatting | bytes 131072 | tf_op jit(solution)/shard_map/reshape | solution.py:514
  65.1 0.1 copy.7
  65.1 0.7 %reshape.15 = f32[8,8,256]{2,1,0:T(8,128)} reshape(f32[64,2,128]{2,1,0:T(2,128)S(1)} %copy.7) | data formatting | bytes 131072 | tf_op jit(solution)/shard_map/reshape | solution.py:514
  (1 shorter events, 0.0 us)
Async XLA Ops:
  0.6 1.0 %copy-start.1 = (s32[8,4096]{1,0:T(8,128)S(1)}, s32[8,4096]{1,0:T(8,128)}, u32[]{:S(2)}) copy-start(s32[8,4096]{1,0:T(8,128)} %ids_hbm.1) | copy-start | bytes 393220
  0.6 1.0 %copy-start = (f32[8,4096]{1,0:T(8,128)S(1)}, f32[8,4096]{1,0:T(8,128)}, u32[]{:S(2)}) copy-start(f32[8,4096]{1,0:T(8,128)} %vec_hbm.1) | copy-start | bytes 393220

commit v2 on v1

--- a/solution.py
+++ b/solution.py
@@ -214,11 +214,11 @@
 
 
 def kernel(
-    planes, scale, vec_hbm, ids_hbm, books_hbm, x_ref, r_ref,
-    vec, books, ids, low, high, e_local, e_rows, fold, acc,
-    rs_out, rs_in, pair_out, pair_in, base, base_in, last_in,
+    planes, scale, vec_hbm, ids_hbm, books_hbm, x_hbm, r_hbm,
+    vec, books, ids, low, high, e_local, e_rows, e_even, e_odd, fold,
+    rs_out, rs_in, pair_out, pair_in, base, base_in, last_in, x_out, r_out,
     z_out, z_in, s_out, s_in,
-    in_sem, ids_send, ids_recv, rs_send, rs_recv, pair_send, pair_recv,
+    in_sem, out_sem, ids_send, ids_recv, rs_send, rs_recv, pair_send, pair_recv,
     ag_send, ag_recv, z_send, z_recv, s_send, s_recv,
 ):
     dp = lax.axis_index("dp")
@@ -239,8 +239,9 @@
 
     inputs = [
         pltpu.make_async_copy(ids_hbm, ids.at[8], in_sem.at[0]),
-        pltpu.make_async_copy(books_hbm, books, in_sem.at[1]),
-        pltpu.make_async_copy(vec_hbm, vec, in_sem.at[2]),
+        pltpu.make_async_copy(vec_hbm, vec, in_sem.at[1]),
+        pltpu.make_async_copy(books_hbm.at[:, 0:LANES], books.at[0], in_sem.at[2]),
+        pltpu.make_async_copy(books_hbm.at[:, LANES:], books.at[1], in_sem.at[3]),
     ]
     for copy in inputs:
         copy.start()
@@ -320,19 +321,20 @@
         pl.when(jnp.logical_not(skip))(act)
 
     inputs[0].wait()
+    pl.semaphore_wait(barrier, 31 + devices - 2)
+    each(1, 16, lambda k: ids_copy(k).start())
+
     make_masks(ids.at[8], low.at[8], high.at[8])
-    inputs[1].wait()
-    inputs[2].wait()
+    for copy in inputs[1:]:
+        copy.wait()
     forward_local(books, vec, ids.at[8], e_local)
     for d in range(8):
         e_rows[d] = e_local[d : d + 1, :]
         for h in range(2):
             rs_out[d, :, h * LANES : (h + 1) * LANES] = (RIDGE / 16) * books[h, pl.ds(d, 8, stride=8), :]
 
-    pl.semaphore_wait(barrier, 31 + devices - 2)
-    each(1, 16, lambda k: ids_copy(k).start())
-
-    def local_pass(d, carry):
+    def local_pass(k, carry):
+        d = (slot + k) % 8
         found = extract(backward(low.at[8], high.at[8], e_rows.at[d]), fold)
         rs_out[d] = scale * found - rs_out[d]
         for other in range(2):
@@ -340,6 +342,20 @@
         return carry
 
     lax.fori_loop(0, 8, local_pass, 0)
+
+    def place(q):
+        return jnp.where(owned, jnp.where(q == 0, 8, (slot + 8 - q) % 8), 7 - q)
+
+    def arrival(q):
+        where = place(q)
+
+        @pl.when(where < 8)
+        def _():
+            ids_arrival(where, 0).wait_recv()
+            ids_arrival(where, 1).wait_recv()
+            make_masks(ids.at[where], low.at[where], high.at[where])
+
+    each(0, 8, arrival)
 
     @pl.when(owned)
     def _():
@@ -360,28 +376,6 @@
         pair_copy(p).wait_recv()
         base[p + 1] = (pair_out[p] + pair_in[p]) + (RIDGE - SHIFT) * base[p]
 
-    def place(q):
-        return jnp.where(jnp.logical_and(owned, q == 0), 8, (slot + q) % 8)
-
-    acc[...] = jnp.zeros_like(acc)
-
-    def first_pass(q, carry):
-        where = place(q)
-
-        @pl.when(where < 8)
-        def _():
-            ids_arrival(where, 0).wait_recv()
-            ids_arrival(where, 1).wait_recv()
-            make_masks(ids.at[where], low.at[where], high.at[where])
-
-        forward(base[0], ids.at[where], e_rows.at[q])
-        acc[...] += backward(low.at[where], high.at[where], e_rows.at[q])
-        return carry
-
-    lax.fori_loop(0, 8, first_pass, 0)
-    join(0, extract(acc[...], fold))
-    joined(0)
-
     def sweep():
         def two(q, total):
             first, second = place(2 * q), place(2 * q + 1)
@@ -391,9 +385,34 @@
 
         return lax.fori_loop(0, 4, two, jnp.zeros((128, CODES), f32))
 
-    each(0, 8, lambda q: forward(base[1], ids.at[place(q)], e_rows.at[q]))
-    join(1, extract(sweep(), fold))
-    joined(1)
+    def ahead(table, q, rows):
+        for u in range(2):
+            forward(table, ids.at[place(2 * q + u)], rows.at[u])
+
+    def behind(q, rows):
+        terms = []
+        for u in range(2):
+            where = place(2 * q + u)
+            terms.append(backward(low.at[where], high.at[where], rows.at[u]))
+        return terms[0] + terms[1]
+
+    def fused(table):
+        ahead(table, 0, e_even)
+
+        def four(t, total):
+            total = total + behind(2 * t, e_even)
+            ahead(table, 2 * t + 1, e_odd)
+            total = total + behind(2 * t + 1, e_odd)
+            ahead(table, (2 * t + 2) % 4, e_even)
+            return total
+
+        return lax.fori_loop(0, 2, four, jnp.zeros((128, CODES), f32))
+
+    def early_pass(p):
+        join(p, extract(fused(base[p]), fold))
+        joined(p)
+
+    each(0, 2, early_pass)
 
     @pl.when(owned)
     def _():
@@ -446,13 +465,27 @@
             lanes = slice(h * LANES, (h + 1) * LANES)
             rows = pl.ds(d, 8, stride=8)
             v0, v1, v2 = [base_in[d, k, :, lanes] for k in range(3)]
-            x_ref[h, rows, :] = books[h, rows, :] + (c0 * v0 + c1 * v1 + c2 * v2)
+            x_out[h, rows, :] = books[h, rows, :] + (c0 * v0 + c1 * v1 + c2 * v2)
             base_in[d, 0, :, lanes] = q0 * v0 + q1 * v1 + q2 * v2
+    def outgoing(which):
+        source, target = ((x_out, x_hbm), (r_out, r_hbm))[which]
+        return [
+            pltpu.make_async_copy(
+                source.at[h], target.at[:, h * LANES : (h + 1) * LANES], out_sem.at[2 * which + h]
+            )
+            for h in range(2)
+        ]
+
+    for copy in outgoing(0):
+        copy.start()
     each(0, 8, lambda r: arrived(1, r))
     for d in range(8):
         for h in range(2):
             lanes = slice(h * LANES, (h + 1) * LANES)
-            r_ref[h, pl.ds(d, 8, stride=8), :] = base_in[d, 0, :, lanes] + q3 * last_in[d, :, lanes]
+            r_out[h, pl.ds(d, 8, stride=8), :] = base_in[d, 0, :, lanes] + q3 * last_in[d, :, lanes]
+
+    for copy in outgoing(1):
+        copy.start()
 
     each(1, 16, lambda k: ids_copy(k).wait_send())
     for other in range(2):
@@ -466,6 +499,9 @@
         each(1, 16, lambda k: ag_copy(0, k).wait_send())
         each(1, 16, lambda k: ag_copy(1, k).wait_send())
 
+    for copy in outgoing(0) + outgoing(1):
+        copy.wait()
+
 
 def per_device(planes, vectors, code_ids, start_books):
     sections, width, codes = start_books.shape
@@ -473,14 +509,15 @@
     scale = codes / (count * 16)
     devices = 2 * planes
     rows = sections * width
-    books = jnp.transpose(start_books.reshape(rows, 2, LANES), (1, 0, 2))
+    books = start_books.reshape(rows, codes)
     dma = pltpu.SemaphoreType.DMA
+    flat = (rows, codes)
     halves = (2, rows, LANES)
     x, r = pl.pallas_call(
         functools.partial(kernel, planes, scale),
-        out_shape=(jax.ShapeDtypeStruct(halves, f32),) * 2,
+        out_shape=(jax.ShapeDtypeStruct(flat, f32),) * 2,
         in_specs=[pl.BlockSpec(memory_space=pl.ANY)] * 3,
-        out_specs=(pl.BlockSpec(memory_space=pltpu.VMEM),) * 2,
+        out_specs=(pl.BlockSpec(memory_space=pl.ANY),) * 2,
         scratch_shapes=[
             pltpu.VMEM((width, count), f32),
             pltpu.VMEM(halves, f32),
@@ -489,8 +526,9 @@
             pltpu.VMEM((9, count, CODES), bf16),
             pltpu.VMEM((width, count), f32),
             pltpu.VMEM((8, 1, count), f32),
+            pltpu.VMEM((2, 1, count), f32),
+            pltpu.VMEM((2, 1, count), f32),
             pltpu.VMEM((64, LANES), f32),
-            pltpu.VMEM((128, CODES), f32),
             pltpu.VMEM((8, sections, CODES), f32),
             pltpu.VMEM((16, sections, CODES), f32),
             pltpu.VMEM((3, sections, CODES), f32),
@@ -498,11 +536,13 @@
             pltpu.VMEM((4, sections, CODES), f32),
             pltpu.VMEM((8, 3, sections, CODES), f32),
             pltpu.VMEM((8, sections, CODES), f32),
+            pltpu.VMEM(halves, f32),
+            pltpu.VMEM(halves, f32),
             pltpu.VMEM((16, LANES), f32),
             pltpu.VMEM((devices, 16, LANES), f32),
             pltpu.VMEM((16, LANES), f32),
             pltpu.VMEM((16, 16, LANES), f32),
-            dma((3,)), dma((16,)), dma((8, 2)), dma((8, 2)), dma((16,)), dma((3,)), dma((3,)),
+            dma((4,)), dma((4,)), dma((16,)), dma((8, 2)), dma((8, 2)), dma((16,)), dma((3,)), dma((3,)),
             dma((2, 16)), dma((2, 8)), dma((devices,)), dma((devices,)), dma((16,)), dma((16,)),
         ],
         compiler_params=pltpu.CompilerParams(
@@ -510,10 +550,7 @@
         ),
     )(vectors, code_ids, books)
 
-    def back(array):
-        return jnp.transpose(array, (1, 0, 2)).reshape(sections, width, codes)
-
-    return back(x), back(r)
+    return x.reshape(sections, width, codes), r.reshape(sections, width, codes)
 
 
 def solution(mesh):

time: 65.9 us -> 59.1 us (0.90)
  Pallas kernels: 62.7 us -> 54.4 us
  local copies, waits for them, and re-layouts: 2.44 us -> 3.9 us
    pallas_call x1, Pallas kernels: 62.7 us -> 54.4 us  [per_device(): pl.pallas_call(functools.partial(kernel, planes, scale), out_shape=(jax.S...]
    unnamed x4 -> x8, local copies, waits for them, and re-layouts: 0.04 us -> 3.9 us
    reshape x4 -> x0, local copies, waits for them, and re-layouts: 2.29 us -> none  [the longest x2 1.37 us: back(): return jnp.transpose(array, (1, 0, 2)).reshape(sections, width, codes)]
where the time goes in v2:
time: 59.1 us; the launch traced here: 58.9 us
  Pallas kernels  54.4 us (92%)
  local copies, waits for them, and re-layouts  3.9 us (7%)
  between operations  0.65 us (1%)
    pallas_call x1, Pallas kernels, per_device(): pl.pallas_call(functools.partial(kernel, planes, scale), out_shape=(jax.S...  54.4 us
    unnamed x8, local copies, waits for them, and re-layouts  3.9 us

profile of v2, /device:TPU:1, one launch (start us, length us, event | category | flops | bytes accessed | tf_op | source)
XLA Modules:
  0.0 58.9 jit_solution(17028262286336175650)
XLA Ops:
  0.6 0.0 copy-start
  0.6 0.9 %copy-done = f32[8,4096]{1,0:T(8,128)S(1)} copy-done((f32[8,4096]{1,0:T(8,128)S(1)}, f32[8,4096]{1,0:T(8,128)}, u32[]{:S(2)}) %copy-start) | copy-done | bytes 131096
  1.5 0.0 copy-start.1
  1.5 0.9 %copy-done.1 = s32[8,4096]{1,0:T(8,128)S(1)} copy-done((s32[8,4096]{1,0:T(8,128)S(1)}, s32[8,4096]{1,0:T(8,128)}, u32[]{:S(2)}) %copy-start.1) | copy-done | bytes 131096
  2.4 0.0 copy-start.2
  2.4 0.8 %copy-done.2 = f32[8,8,256]{2,1,0:T(8,128)S(1)} copy-done((f32[8,8,256]{2,1,0:T(8,128)S(1)}, f32[8,8,256]{2,1,0:T(8,128)}, u32[]{:S(2)}) %copy-start.2) | copy-done | bytes 65560
  3.3 54.4 %shard_map.50 = (f32[64,256]{1,0:T(8,128)S(1)}, f32[64,256]{1,0:T(8,128)S(1)}) custom-call(f32[8,4096]{1,0:T(8,128)S(1)} %copy-done, s32[8,4096]{1,0:T(8,128)S(1)} %copy-done.1, f32[64,256]{1,0:T(8,128)S(1)} %bitcast.3), custom_call_target="tpu_custom_call" | custom-call | tf_op jit(solution)/shard_map/pallas_call | solution.py:516
  57.6 0.6 %copy.7 = f32[8,8,256]{2,1,0:T(8,128)} copy(f32[8,8,256]{2,1,0:T(8,128)S(1)} %bitcast.5) | data formatting | bytes 131072
  58.3 0.6 %copy.8 = f32[8,8,256]{2,1,0:T(8,128)} copy(f32[8,8,256]{2,1,0:T(8,128)S(1)} %bitcast.4) | data formatting | bytes 131072
Async XLA Ops:
  0.6 0.9 %copy-start = (f32[8,4096]{1,0:T(8,128)S(1)}, f32[8,4096]{1,0:T(8,128)}, u32[]{:S(2)}) copy-start(f32[8,4096]{1,0:T(8,128)} %vec_hbm.1) | copy-start | bytes 393220
  1.5 0.9 %copy-start.1 = (s32[8,4096]{1,0:T(8,128)S(1)}, s32[8,4096]{1,0:T(8,128)}, u32[]{:S(2)}) copy-start(s32[8,4096]{1,0:T(8,128)} %ids_hbm.1) | copy-start | bytes 393220
  2.4 0.8 %copy-start.2 = (f32[8,8,256]{2,1,0:T(8,128)S(1)}, f32[8,8,256]{2,1,0:T(8,128)}, u32[]{:S(2)}) copy-start(f32[8,8,256]{2,1,0:T(8,128)} %param.5) | copy-start | bytes 196612

commit v3 on v2

--- a/solution.py
+++ b/solution.py
@@ -15,6 +15,17 @@
 CODES = 256
 RIDGE = 0.5
 SHIFT = 2.0
+EVEN = ((0, 0), (1, 1), (3, 3), (1, 3), (3, 1), (0, 2), (2, 0), (2, 2))
+ODD = ((0, 1), (0, 3), (1, 0), (3, 0), (2, 1), (2, 3), (1, 2), (3, 2))
+MOVES = tuple(move for pair in zip(ODD, EVEN[1:]) for move in pair) + (ODD[7],)
+EARLY = 6
+
+
+def entry(table, k, which):
+    out = jnp.int32(table[0][which])
+    for place in range(1, len(table)):
+        out = jnp.where(k == place, table[place][which], out)
+    return out
 
 
 def two_sum(a, b):
@@ -225,9 +236,11 @@
     dim = lax.axis_index("dim")
     core = dim % 2
     plane = dim // 2
-    owner = dp // 8
-    slot = dp % 8
+    y, x = dp // 4, dp % 4
+    owner, slot = dp // 8, dp % 8
     owned = core == owner
+    keeper = (y + x) % 2
+    kept = core == keeper
     half = ids.shape[2] // 2
     devices = 2 * planes
 
@@ -266,8 +279,8 @@
 
     def ids_copy(k):
         return remote(
-            ids_part(8, core), ids_part(slot, core), ids_send.at[k], ids_recv.at[slot, core],
-            ((dp + k) % 16, 2 * plane + owner),
+            ids_part(8, core), ids_part((k + 1) // 2, core), ids_send.at[k], ids_recv.at[(k + 1) // 2, core],
+            ((y + entry(MOVES, k, 0)) % 4 * 4 + (x + entry(MOVES, k, 1)) % 4, 2 * plane + keeper),
         )
 
     def ids_arrival(where, which):
@@ -322,7 +335,7 @@
 
     inputs[0].wait()
     pl.semaphore_wait(barrier, 31 + devices - 2)
-    each(1, 16, lambda k: ids_copy(k).start())
+    each(0, 5, lambda k: ids_copy(k).start())
 
     make_masks(ids.at[8], low.at[8], high.at[8])
     for copy in inputs[1:]:
@@ -333,18 +346,21 @@
         for h in range(2):
             rs_out[d, :, h * LANES : (h + 1) * LANES] = (RIDGE / 16) * books[h, pl.ds(d, 8, stride=8), :]
 
+    each(5, 7, lambda k: ids_copy(k).start())
+
     def local_pass(k, carry):
         d = (slot + k) % 8
         found = extract(backward(low.at[8], high.at[8], e_rows.at[d]), fold)
         rs_out[d] = scale * found - rs_out[d]
         for other in range(2):
             pl.when(rs_away(d, other))(lambda: rs_copy(d, other).start())
+        ids_copy(7 + k).start()
         return carry
 
     lax.fori_loop(0, 8, local_pass, 0)
 
     def place(q):
-        return jnp.where(owned, jnp.where(q == 0, 8, (slot + 8 - q) % 8), 7 - q)
+        return jnp.where(jnp.logical_and(kept, q == 0), 8, q)
 
     def arrival(q):
         where = place(q)
@@ -355,7 +371,7 @@
             ids_arrival(where, 1).wait_recv()
             make_masks(ids.at[where], low.at[where], high.at[where])
 
-    each(0, 8, arrival)
+    each(0, EARLY, arrival)
 
     @pl.when(owned)
     def _():
@@ -408,25 +424,33 @@
 
         return lax.fori_loop(0, 2, four, jnp.zeros((128, CODES), f32))
 
-    def early_pass(p):
-        join(p, extract(fused(base[p]), fold))
-        joined(p)
-
-    each(0, 2, early_pass)
+    def first(t, total):
+        @pl.when(2 * t >= EARLY)
+        def _():
+            arrival(2 * t)
+            arrival(2 * t + 1)
+
+        ahead(base[0], t, e_even)
+        return total + behind(t, e_even)
+
+    join(0, extract(lax.fori_loop(0, 4, first, jnp.zeros((128, CODES), f32)), fold))
+    joined(0)
+    join(1, extract(fused(base[1]), fold))
+    joined(1)
 
     @pl.when(owned)
     def _():
         each(1, 16, lambda k: ag_copy(0, k).start())
         base_in[slot] = base[0:3]
 
-    def last_forward(q, carry):
-        blocks = forward(base[2], ids.at[place(q)], e_rows.at[q], packed=True)
-        for block in blocks:
-            carry = plus(carry, two_prod(block, block))
-        return carry
+    def last_forward(t, carry):
+        blocks = []
+        for q in (2 * t, 2 * t + 1):
+            blocks += forward(base[2], ids.at[place(q)], e_rows.at[q], packed=True)
+        return plus(carry, tree([two_prod(block, block) for block in blocks]))
 
     zero = jnp.zeros((8, LANES), f32)
-    norm = lax.fori_loop(0, 8, last_forward, (zero, zero))
+    norm = lax.fori_loop(0, 4, last_forward, (zero, zero))
     v0, v1, v2 = base[0], base[1], base[2]
     sums = dot_rows([(v0, v0), (v0, v1), (v0, v2), (v1, v1), (v1, v2), (v2, v2)], norm)
     z_out[0:8] = sums[0]
@@ -487,7 +511,7 @@
     for copy in outgoing(1):
         copy.start()
 
-    each(1, 16, lambda k: ids_copy(k).wait_send())
+    each(0, 15, lambda k: ids_copy(k).wait_send())
     for other in range(2):
         each(0, 8, lambda d: pl.when(rs_away(d, other))(lambda: rs_copy(d, other).wait_send()))
     each(0, 3, lambda p: pair_copy(p).wait_send())
@@ -546,7 +570,7 @@
             dma((2, 16)), dma((2, 8)), dma((devices,)), dma((devices,)), dma((16,)), dma((16,)),
         ],
         compiler_params=pltpu.CompilerParams(
-            collective_id=0, has_side_effects=True, vmem_limit_bytes=48 << 20
+            collective_id=0, has_side_effects=True, vmem_limit_bytes=61 << 20
         ),
     )(vectors, code_ids, books)
 

time: 59.1 us -> 55.9 us (0.946)
  local copies, waits for them, and re-layouts: 3.9 us -> 2.14 us
  Pallas kernels: 54.4 us -> 53 us
    unnamed x8 -> x4, local copies, waits for them, and re-layouts: 3.9 us -> 2.14 us
    pallas_call x1, Pallas kernels: 54.4 us -> 53 us  [per_device(): pl.pallas_call(functools.partial(kernel, planes, scale), out_shape=(jax.S...]
where the time goes in v3:
time: 55.9 us; the launch traced here: 55.8 us
  Pallas kernels  53 us (95%)
  local copies, waits for them, and re-layouts  2.14 us (4%)
  between operations  0.65 us (1%)
    pallas_call x1, Pallas kernels, per_device(): pl.pallas_call(functools.partial(kernel, planes, scale), out_shape=(jax.S...  53 us
    unnamed x4, local copies, waits for them, and re-layouts  2.14 us

profile of v3, /device:TPU:1, one launch (start us, length us, event | category | flops | bytes accessed | tf_op | source)
XLA Modules:
  0.0 55.8 jit_solution(16420557618722201646)
XLA Ops:
  0.6 53.0 %shard_map.50 = (f32[64,256]{1,0:T(8,128)}, f32[64,256]{1,0:T(8,128)}) custom-call(f32[8,4096]{1,0:T(8,128)} %vec_hbm.1, s32[8,4096]{1,0:T(8,128)} %ids_hbm.1, f32[64,256]{1,0:T(8,128)} %bitcast.3), custom_call_target="tpu_custom_call" | custom-call | tf_op jit(solution)/shard_map/pallas_call | solution.py:540
  53.6 0.0 copy-start
  53.6 1.5 %copy.7 = f32[8,8,256]{2,1,0:T(8,128)} copy(f32[8,8,256]{2,1,0:T(8,128)} %bitcast.5) | data formatting | bytes 131072
  55.1 0.0 copy-done
  55.1 0.6 %copy.8 = f32[8,8,256]{2,1,0:T(8,128)} copy(f32[8,8,256]{2,1,0:T(8,128)S(1)} %bitcast.4) | data formatting | bytes 131072
Async XLA Ops:
  53.6 1.5 %copy-start = (f32[64,256]{1,0:T(8,128)S(1)}, f32[64,256]{1,0:T(8,128)}, u32[]{:S(2)}) copy-start(f32[64,256]{1,0:T(8,128)} %get-tuple-element.5) | copy-start | bytes 196612

commit v4 on v3

--- a/solution.py
+++ b/solution.py
@@ -22,6 +22,8 @@
 
 
 def entry(table, k, which):
+    if isinstance(k, int):
+        return table[k][which]
     out = jnp.int32(table[0][which])
     for place in range(1, len(table)):
         out = jnp.where(k == place, table[place][which], out)
@@ -81,7 +83,7 @@
     return jnp.where(index >= LANES, high, low)
 
 
-def make_masks(ids_ref, low_ref, high_ref, chunk=1024):
+def make_masks(ids_ref, low_ref, high_ref, chunk=2048):
     count = ids_ref.shape[1]
     row_low = lax.broadcasted_iota(jnp.int32, (64, chunk), 0) & 7
     row_high = lax.broadcasted_iota(jnp.int32, (CODES, chunk), 0) & 31
@@ -118,7 +120,7 @@
         e_ref[:, span] = total
         return carry
 
-    lax.fori_loop(0, count // LANES, step, 0, unroll=4)
+    lax.fori_loop(0, count // LANES, step, 0, unroll=8)
 
 
 def forward(table, ids_ref, e_ref, packed=False):
@@ -175,22 +177,23 @@
     return jnp.concatenate(halves, axis=1)
 
 
-def dot_rows(pairs, extra):
+def dots(pairs, first, carry, extra=()):
     row = lax.broadcasted_iota(jnp.int32, (8, LANES), 0)
     found = []
     for a, b in pairs:
         left = two_prod(a[:, :LANES], b[:, :LANES])
         right = two_prod(a[:, LANES:], b[:, LANES:])
         found.append(scaled(plus(left, right), 0.5))
-    found.append(extra)
-    high = jnp.zeros((8, LANES), f32)
-    rest = jnp.zeros((8, LANES), f32)
-    for q, pair in enumerate(found):
+    high, rest = carry
+    for q, pair in enumerate(found + list(extra)):
         for distance in (4, 2, 1):
             pair = plus(pair, (pltpu.roll(pair[0], distance, 0), pltpu.roll(pair[1], distance, 0)))
-        high = jnp.where(row == q, pair[0], high)
-        rest = jnp.where(row == q, pair[1], rest)
-    pair = (high, rest)
+        high = jnp.where(row == first + q, pair[0], high)
+        rest = jnp.where(row == first + q, pair[1], rest)
+    return high, rest
+
+
+def over_lanes(pair):
     for distance in (64, 32, 16, 8, 4, 2, 1):
         pair = plus(pair, (pltpu.roll(pair[0], distance, 1), pltpu.roll(pair[1], distance, 1)))
     return pair
@@ -203,7 +206,7 @@
 
 
 def solve(total, scale):
-    d00, d01, d02, d11, d12, d22, norm = [(total[0][q : q + 1], total[1][q : q + 1]) for q in range(7)]
+    d00, d01, d11, d02, d12, d22, norm = [(total[0][q : q + 1], total[1][q : q + 1]) for q in range(7)]
     w00 = plus(d01, scaled(d00, SHIFT))
     w01 = plus(d02, scaled(d01, SHIFT))
     w02 = plus(d12, scaled(d02, SHIFT))
@@ -335,7 +338,8 @@
 
     inputs[0].wait()
     pl.semaphore_wait(barrier, 31 + devices - 2)
-    each(0, 5, lambda k: ids_copy(k).start())
+    for k in range(7):
+        ids_copy(k).start()
 
     make_masks(ids.at[8], low.at[8], high.at[8])
     for copy in inputs[1:]:
@@ -346,7 +350,6 @@
         for h in range(2):
             rs_out[d, :, h * LANES : (h + 1) * LANES] = (RIDGE / 16) * books[h, pl.ds(d, 8, stride=8), :]
 
-    each(5, 7, lambda k: ids_copy(k).start())
 
     def local_pass(k, carry):
         d = (slot + k) % 8
@@ -436,12 +439,10 @@
     join(0, extract(lax.fori_loop(0, 4, first, jnp.zeros((128, CODES), f32)), fold))
     joined(0)
     join(1, extract(fused(base[1]), fold))
+    zero = jnp.zeros((8, LANES), f32)
+    v0, v1 = base[0], base[1]
+    sums = dots([(v0, v0), (v0, v1), (v1, v1)], 0, (zero, zero))
     joined(1)
-
-    @pl.when(owned)
-    def _():
-        each(1, 16, lambda k: ag_copy(0, k).start())
-        base_in[slot] = base[0:3]
 
     def last_forward(t, carry):
         blocks = []
@@ -449,14 +450,19 @@
             blocks += forward(base[2], ids.at[place(q)], e_rows.at[q], packed=True)
         return plus(carry, tree([two_prod(block, block) for block in blocks]))
 
-    zero = jnp.zeros((8, LANES), f32)
     norm = lax.fori_loop(0, 4, last_forward, (zero, zero))
-    v0, v1, v2 = base[0], base[1], base[2]
-    sums = dot_rows([(v0, v0), (v0, v1), (v0, v2), (v1, v1), (v1, v2), (v2, v2)], norm)
+    v2 = base[2]
+    sums = over_lanes(dots([(v0, v2), (v1, v2), (v2, v2)], 3, sums, [norm]))
     z_out[0:8] = sums[0]
     z_out[8:16] = sums[1]
     each(1, devices, lambda k: z_copy(k).start())
     z_in[dim] = z_out[...]
+
+    @pl.when(owned)
+    def _():
+        each(1, 16, lambda k: ag_copy(0, k).start())
+        base_in[slot] = base[0:3]
+
     join(2, extract(sweep(), fold))
     each(0, devices, lambda k: unless(k == dim, lambda: z_arrival(k).wait_recv()))
     sums = tree([(z_in[k, 0:8], z_in[k, 8:16]) for k in range(devices)])

time: 55.9 us -> 54.5 us (0.975)
  Pallas kernels: 53 us -> 51.6 us
    pallas_call x1, Pallas kernels: 53 us -> 51.6 us  [per_device(): pl.pallas_call(functools.partial(kernel, planes, scale), out_shape=(jax.S...]
where the time goes in v4:
time: 54.5 us; the launch traced here: 54.3 us
  Pallas kernels  51.6 us (95%)
  local copies, waits for them, and re-layouts  2.14 us (4%)
  between operations  0.65 us (1%)
    pallas_call x1, Pallas kernels, per_device(): pl.pallas_call(functools.partial(kernel, planes, scale), out_shape=(jax.S...  51.6 us
    unnamed x4, local copies, waits for them, and re-layouts  2.14 us

profile of v4, /device:TPU:1, one launch (start us, length us, event | category | flops | bytes accessed | tf_op | source)
XLA Modules:
  0.0 54.3 jit_solution(5499487329740744537)
XLA Ops:
  0.6 51.6 %shard_map.50 = (f32[64,256]{1,0:T(8,128)}, f32[64,256]{1,0:T(8,128)}) custom-call(f32[8,4096]{1,0:T(8,128)} %vec_hbm.1, s32[8,4096]{1,0:T(8,128)} %ids_hbm.1, f32[64,256]{1,0:T(8,128)} %bitcast.3), custom_call_target="tpu_custom_call" | custom-call | tf_op jit(solution)/shard_map/pallas_call | solution.py:546
  52.2 0.0 copy-start
  52.2 1.5 %copy.7 = f32[8,8,256]{2,1,0:T(8,128)} copy(f32[8,8,256]{2,1,0:T(8,128)} %bitcast.5) | data formatting | bytes 131072
  53.7 0.0 copy-done
  53.7 0.6 %copy.8 = f32[8,8,256]{2,1,0:T(8,128)} copy(f32[8,8,256]{2,1,0:T(8,128)S(1)} %bitcast.4) | data formatting | bytes 131072
Async XLA Ops:
  52.2 1.5 %copy-start = (f32[64,256]{1,0:T(8,128)S(1)}, f32[64,256]{1,0:T(8,128)}, u32[]{:S(2)}) copy-start(f32[64,256]{1,0:T(8,128)} %get-tuple-element.5) | copy-start | bytes 196612

commit v5 on v4

--- a/solution.py
+++ b/solution.py
@@ -264,18 +264,13 @@
 
     barrier = pltpu.get_barrier_semaphore()
 
-    def greet_plane(k, carry):
-        target = ((dp + k // 2) % 16, 2 * plane + (core + k) % 2)
+    for k in range(2, devices):
+        target = (dp, 2 * lax.rem(plane + k // 2, planes) + k % 2)
         pl.semaphore_signal(barrier, inc=1, device_id=target, device_id_type=MESH)
-        return carry
-
-    def greet_line(k, carry):
-        target = (dp, 2 * ((plane + k // 2) % planes) + k % 2)
+    for k in range(1, 32):
+        target = (lax.rem(dp + k // 2, 16), 2 * plane + lax.rem(core + k, 2))
         pl.semaphore_signal(barrier, inc=1, device_id=target, device_id_type=MESH)
-        return carry
-
-    lax.fori_loop(1, 32, greet_plane, 0)
-    lax.fori_loop(2, devices, greet_line, 0)
+
 
     def ids_part(where, which):
         return ids.at[where, :, pl.ds(pl.multiple_of(which * half, half), half)]
@@ -307,7 +302,7 @@
         )
 
     def ag_copy(which, k):
-        target = ((dp + k) % 16, dim)
+        target = (lax.rem(dp + k, 16), dim)
         if which == 0:
             return remote(base.at[pl.ds(0, 3)], base_in.at[slot], ag_send.at[0, k], ag_recv.at[0, slot], target)
         return remote(base.at[3], last_in.at[slot], ag_send.at[1, k], ag_recv.at[1, slot], target)
@@ -319,13 +314,13 @@
         return remote(base.at[3], last_in.at[r], ag_send.at[1, 0], ag_recv.at[1, r], target)
 
     def z_copy(k):
-        return remote(z_out, z_in.at[dim], z_send.at[k], z_recv.at[dim], (dp, (dim + k) % devices))
+        return remote(z_out, z_in.at[dim], z_send.at[k], z_recv.at[dim], (dp, lax.rem(dim + k, devices)))
 
     def z_arrival(k):
         return remote(z_out, z_in.at[k], z_send.at[0], z_recv.at[k], (dp, (dim + 1) % devices))
 
     def s_copy(k):
-        return remote(s_out, s_in.at[dp], s_send.at[k], s_recv.at[dp], ((dp + k) % 16, dim))
+        return remote(s_out, s_in.at[dp], s_send.at[k], s_recv.at[dp], (lax.rem(dp + k, 16), dim))
 
     def s_arrival(k):
         return remote(s_out, s_in.at[k], s_send.at[0], s_recv.at[k], ((dp + 1) % 16, dim))

time: 54.5 us -> 54.2 us (level)
  no operation moved by 1% of the time
where the time goes in v5:
time: 54.2 us; the launch traced here: 54.1 us
  Pallas kernels  51.3 us (95%)
  local copies, waits for them, and re-layouts  2.14 us (4%)
  between operations  0.65 us (1%)
    pallas_call x1, Pallas kernels, per_device(): pl.pallas_call(functools.partial(kernel, planes, scale), out_shape=(jax.S...  51.3 us
    unnamed x4, local copies, waits for them, and re-layouts  2.14 us

profile of v5, /device:TPU:1, one launch (start us, length us, event | category | flops | bytes accessed | tf_op | source)
XLA Modules:
  0.0 54.1 jit_solution(15872120057643290022)
XLA Ops:
  0.6 51.3 %shard_map.50 = (f32[64,256]{1,0:T(8,128)}, f32[64,256]{1,0:T(8,128)}) custom-call(f32[8,4096]{1,0:T(8,128)} %vec_hbm.1, s32[8,4096]{1,0:T(8,128)} %ids_hbm.1, f32[64,256]{1,0:T(8,128)} %bitcast.3), custom_call_target="tpu_custom_call" | custom-call | tf_op jit(solution)/shard_map/pallas_call | solution.py:541
  51.9 0.0 copy-start
  52.0 1.5 %copy.7 = f32[8,8,256]{2,1,0:T(8,128)} copy(f32[8,8,256]{2,1,0:T(8,128)} %bitcast.5) | data formatting | bytes 131072
  53.5 0.0 copy-done
  53.5 0.6 %copy.8 = f32[8,8,256]{2,1,0:T(8,128)} copy(f32[8,8,256]{2,1,0:T(8,128)S(1)} %bitcast.4) | data formatting | bytes 131072
Async XLA Ops:
  51.9 1.5 %copy-start = (f32[64,256]{1,0:T(8,128)S(1)}, f32[64,256]{1,0:T(8,128)}, u32[]{:S(2)}) copy-start(f32[64,256]{1,0:T(8,128)} %get-tuple-element.5) | copy-start | bytes 196612
